TPU v7x, 32 devices: a whole 2x2x4 slice. The times are simulated.
32 devices in a mesh: row: 4 (over y, x), col: 8 (over z, core).
Axes of the slice: x: 2, y: 2, z: 4, core: 2. Of those that a mesh axis runs over, the one named last changes fastest.
Arguments:
- grad_out: bfloat16 [4096, 8192], P('col', 'row'), may hold values from -4 to 4
- proj_weight: bfloat16 [8192, 4096], P('col', 'row'), may hold values from -0.09375 to 0.09375
- queries: bfloat16 [4096, 4096], P('col', 'row'), may hold values from -5 to 5
- keys: bfloat16 [4096, 4096], P('col', 'row'), may hold values from -5 to 5
- values: bfloat16 [4096, 4096], P('col', 'row'), may hold values from -6 to 6
- cache_keys: bfloat16 [1024, 4096], P('col', 'row'), may hold values from -6 to 6
- cache_values: bfloat16 [1024, 4096], P('col', 'row'), may hold values from -6 to 6
- block_table: int32 [32, 4], P('col'), may hold values from 0 to 7, all different within a row
Outputs:
- grad_q: bfloat16 [4096, 4096], P('col', 'row')
- grad_k: bfloat16 [4096, 4096], P('col', 'row')
- grad_v: bfloat16 [4096, 4096], P('col', 'row')
- grad_cache_k: float32 [1024, 4096], P('col', 'row')
- grad_cache_v: float32 [1024, 4096], P('col', 'row')
- grad_weight: bfloat16 [8192, 4096], P('col', 'row')
Inputs may be any that keep to these rules, and one draw needn't show every extreme that they name: `block_table`: each row names 4 different cached blocks, and every cached block is named by some row.
All inputs are finite; a program needn't handle non-finite values.
Results may differ from a plain program's by a relative error of at most 0.023.
Values may be sent and summed in bfloat16 or wider, within the bound.
A program may use at most 128 MiB of HBM per device.

v0:
```python
import math

import jax
import jax.numpy as jnp
from jax import lax
from jax.sharding import PartitionSpec as P

HEAD_DIM = 128
BLOCK = 128
CB = 8
KB = 4
CACHE = 1024


def per_device(grad_out, proj_weight, queries, keys, values, cache_keys, cache_values, block_table):
    tok_rows = grad_out.shape[0]
    local_width = queries.shape[1]
    head_count = local_width // HEAD_DIM
    inverse_root = 1.0 / math.sqrt(HEAD_DIM)
    full_grads = lax.all_gather(grad_out, "row", axis=1, tiled=True)
    columns = full_grads
    grad_sum = jnp.dot(
        columns,
        lax.all_gather(proj_weight, "col", axis=0, tiled=True),
        preferred_element_type=jnp.float32,
    )
    grad_attn = grad_sum.astype(jnp.bfloat16)
    cache_k_all, cache_v_all = (
        lax.all_gather(cache_keys, "col", axis=0, tiled=True),
        lax.all_gather(cache_values, "col", axis=0, tiled=True),
    )
    cache_key_blocks = cache_k_all.reshape(CB, BLOCK, head_count, HEAD_DIM)
    cache_value_blocks = cache_v_all.reshape(CB, BLOCK, head_count, HEAD_DIM)
    blocks_here = tok_rows // BLOCK
    group = math.gcd(blocks_here, max(1, 512 // BLOCK))
    turns = blocks_here // group
    positions = jnp.arange(BLOCK, dtype=jnp.int32)
    causal = positions[:, None] >= positions[None, :]
    allowed = jnp.concatenate([jnp.ones((BLOCK, KB * BLOCK), dtype=bool), causal], axis=1)
    block_ids = jnp.arange(CB, dtype=jnp.int32)

    def to_groups(array):
        return array.reshape(turns, group, BLOCK, head_count, HEAD_DIM)

    def one_group(carry, inputs):
        grad_ck, grad_cv = carry
        query, own_keys, own_values, grad_block, chosen = inputs
        picked_keys = cache_key_blocks[chosen].reshape(group, KB * BLOCK, head_count, HEAD_DIM)
        picked_values = cache_value_blocks[chosen].reshape(group, KB * BLOCK, head_count, HEAD_DIM)
        key_list = jnp.concatenate([picked_keys, own_keys], axis=1)
        value_list = jnp.concatenate([picked_values, own_values], axis=1)
        scores = (
            jnp.einsum("gqhd,gkhd->ghqk", query, key_list, preferred_element_type=jnp.float32)
            * inverse_root
        )
        scores = jnp.where(allowed[None, None], scores, -jnp.inf)
        row_max = jnp.max(scores, axis=-1, keepdims=True)
        weights = jnp.exp(scores - row_max)
        probs = weights / jnp.sum(weights, axis=-1, keepdims=True)
        probs_b = probs.astype(jnp.bfloat16)
        attn_full = jnp.einsum(
            "ghqk,gkhd->gqhd", probs_b, value_list, preferred_element_type=jnp.float32
        )
        grad_probs = jnp.einsum(
            "gqhd,gkhd->ghqk", grad_block, value_list, preferred_element_type=jnp.float32
        )
        delta = jnp.sum(grad_block.astype(jnp.float32) * attn_full, axis=-1)
        delta = jnp.transpose(delta, (0, 2, 1))[..., None]
        grad_scores = (probs * (grad_probs - delta)).astype(jnp.bfloat16)
        grad_query = (
            jnp.einsum("ghqk,gkhd->gqhd", grad_scores, key_list, preferred_element_type=jnp.float32)
            * inverse_root
        )
        grad_key_list = (
            jnp.einsum("ghqk,gqhd->gkhd", grad_scores, query, preferred_element_type=jnp.float32)
            * inverse_root
        )
        grad_value_list = jnp.einsum(
            "ghqk,gqhd->gkhd", probs_b, grad_block, preferred_element_type=jnp.float32
        )
        one_hot = (chosen.reshape(group * KB)[:, None] == block_ids[None, :]).astype(jnp.float32)
        cache_key_part = grad_key_list[:, : KB * BLOCK].reshape(group * KB, BLOCK * local_width)
        cache_value_part = grad_value_list[:, : KB * BLOCK].reshape(group * KB, BLOCK * local_width)
        grad_ck = grad_ck + jnp.dot(one_hot.T, cache_key_part, precision=lax.Precision.HIGHEST)
        grad_cv = grad_cv + jnp.dot(one_hot.T, cache_value_part, precision=lax.Precision.HIGHEST)
        outputs = (
            grad_query.astype(jnp.bfloat16),
            grad_key_list[:, KB * BLOCK :].astype(jnp.bfloat16),
            grad_value_list[:, KB * BLOCK :].astype(jnp.bfloat16),
            attn_full.astype(jnp.bfloat16),
        )
        return ((grad_ck, grad_cv), outputs)

    start_carry = (
        jnp.zeros((CB, BLOCK * local_width), jnp.float32),
        jnp.zeros((CB, BLOCK * local_width), jnp.float32),
    )
    inputs = (
        to_groups(queries),
        to_groups(keys),
        to_groups(values),
        to_groups(grad_attn),
        block_table.reshape(turns, group, KB),
    )
    (grad_ck, grad_cv), outputs = lax.scan(one_group, start_carry, inputs)
    grad_q = outputs[0].reshape(tok_rows, local_width)
    grad_k = outputs[1].reshape(tok_rows, local_width)
    grad_v = outputs[2].reshape(tok_rows, local_width)
    attn_out = outputs[3].reshape(tok_rows, local_width)
    grad_cache_k, grad_cache_v = (
        lax.psum_scatter(
            grad_ck.reshape(CACHE, local_width).astype(jnp.bfloat16),
            "col",
            scatter_dimension=0,
            tiled=True,
        ).astype(jnp.float32),
        lax.psum_scatter(
            grad_cv.reshape(CACHE, local_width).astype(jnp.bfloat16),
            "col",
            scatter_dimension=0,
            tiled=True,
        ).astype(jnp.float32),
    )
    columns = full_grads
    grad_weight = lax.psum_scatter(
        lax.dot_general(
            columns, attn_out, (((0,), (0,)), ((), ())), preferred_element_type=jnp.float32
        ).astype(jnp.bfloat16),
        "col",
        scatter_dimension=0,
        tiled=True,
    )
    return (grad_q, grad_k, grad_v, grad_cache_k, grad_cache_v, grad_weight)


def solution(mesh):
    in_specs = (
        P("col", "row"),
        P("col", "row"),
        P("col", "row"),
        P("col", "row"),
        P("col", "row"),
        P("col", "row"),
        P("col", "row"),
        P("col", None),
    )
    out_specs = (
        P("col", "row"),
        P("col", "row"),
        P("col", "row"),
        P("col", "row"),
        P("col", "row"),
        P("col", "row"),
    )
    return jax.shard_map(
        per_device, mesh=mesh, in_specs=in_specs, out_specs=out_specs, check_vma=False
    )
```

profile of v0, /device:TPU:0, one launch (start us, length us, event | category | flops | bytes accessed | tf_op | source)
XLA Modules:
  0.0 626.0 jit_solution(1271582533404550745)
XLA Ops:
  15.6 25.8 %all-gather.5.cloned.1.call-done = bf16[1024,1024]{1,0:T(8,128)(2,1)} async-done(((bf16[128,1024]{1,0:T(8,128)(2,1)}), bf16[1024,1024]{1,0:T(8,128)(2,1)}) %all-gather.5.cloned.1.call-update) | async-done | bytes 2097168 | tf_op jit(solution)/shard_map/all_gather | solution.py:29
  43.7 28.0 %all-gather.11.cloned.1.call-done = bf16[1024,1024]{1,0:T(8,128)(2,1)} async-done(((bf16[128,1024]{1,0:T(8,128)(2,1)}), bf16[1024,1024]{1,0:T(8,128)(2,1)}) %all-gather.11.cloned.1.call-update) | async-done | bytes 2097168 | tf_op jit(solution)/shard_map/all_gather | solution.py:30
  78.3 4.9 gather_fusion.1
  92.0 5.3 fusion.12
  97.4 11.1 %fusion.18 = (f32[4,8,128]{2,1,0:T(8,128)S(1)}, f32[4,8,128,640]{2,3,1,0:T(8,128)S(1)}) fusion(f32[4,8,640,128]{3,2,1,0:T(8,128)} %fusion.12, pred[128,640]{0,1:T(8,128)(4,1)S(1)} %concatenate.12), kind=kOutput, calls=%fused_computation.46 | output fusion | flops 15729279 | bytes 21069824 | tf_op jit(solution)/shard_map/while/body/eval_jaxpr/sub | solution.py:58
  108.5 3.9 copy-done.5
  112.4 3.9 fusion.5
  116.3 44.4 %all-gather.7.cloned.1.call-done = bf16[512,8192]{1,0:T(8,128)(2,1)} async-done(((bf16[512,2048]{1,0:T(8,128)(2,1)}), bf16[512,8192]{1,0:T(8,128)(2,1)}) %all-gather.7.cloned.1.call-update) | async-done | bytes 8388624 | tf_op jit(solution)/shard_map/all_gather | solution.py:20
  160.7 152.6 %all-gather.9.cloned.1.call-done = bf16[8192,1024]{1,0:T(8,128)(2,1)} async-done(((bf16[1024,1024]{1,0:T(8,128)(2,1)}), bf16[8192,1024]{1,0:T(8,128)(2,1)}) %all-gather.9.cloned.1.call-update) | async-done | bytes 16777232 | tf_op jit(solution)/shard_map/all_gather | solution.py:24
  313.3 14.8 %fusion.7 = bf16[64,8,8,128]{3,1,2,0:T(8,128)(2,1)S(1)} fusion(bf16[512,8192]{1,0:T(8,128)(2,1)} %all-gather.7.cloned.1.call-done, bf16[8192,1024]{1,0:T(8,128)(2,1)} %all-gather.9.cloned.1.call-done), kind=kOutput, calls=%fused_computation.26 | convolution fusion | flops 8590458880 | bytes 26214400 | tf_op jit(solution)/shard_map/dot_general | solution.py:22
  329.3 6.9 %fusion.6 = (f32[4,128,8]{1,2,0:T(8,128)S(1)}, bf16[4,8,128,128]{3,2,1,0:T(8,128)(2,1)}) fusion(bf16[4,128,8,128]{1,3,2,0:T(8,128)(2,1)S(1)} %copy.32, bf16[4,640,8,128]{3,1,2,0:T(8,128)(2,1)} %copy_dynamic-update-slice_fusion.2, bf16[4,8,128,640]{2,3,1,0:T(8,128)(2,1)} %fusion.5), kind=kOutput, calls=%fused_computation.23 | convolution fusion | flops 673181696 | bytes 12599296 | tf_op jit(solution)/shard_map/while/body/eval_jaxpr/ghqk,gkhd->gqhd/dot_general | solution.py:61
  336.3 7.2 %multiply_convert_fusion = bf16[4,8,128,640]{2,3,1,0:T(8,128)(2,1)S(1)} fusion(f32[4,8,128]{2,1,0:T(8,128)S(1)} %bitcast.104, f32[4,8,128,640]{2,3,1,0:T(8,128)} %copy-done.5, f32[4,8,128]{2,1,0:T(8,128)S(1)} %get-tuple-element.66, bf16[4,640,8,128]{3,1,2,0:T(8,128)(2,1)} %copy_dynamic-update-slice_fusion.2, bf16[4,128,8,128]{1,3,2,0:T(8,128)(2,1)S(1)} %copy.32), kind=kOutput, calls=%fused_computation.8 | convolution fusion | flops 681574400 | bytes 22052864 | tf_op jit(solution)/shard_map/while/body/eval_jaxpr/gqhd,gkhd->ghqk/dot_general | solution.py:64
  351.2 8.2 %copy.44 = f32[4,512,8,128]{3,2,1,0:T(8,128)} copy(f32[4,512,8,128]{3,1,2,0:T(8,128)S(1)} %slice.28) | data formatting | bytes 16777216 | tf_op jit(solution)/shard_map/while/body/eval_jaxpr/slice | solution.py:82
  359.4 6.3 reshape.79
  365.6 6.2 convolution_convert_fusion.1
  374.2 4.5 convolution_bitcast_fusion
  382.5 4.3 slice.29
  386.8 9.9 %copy.45 = f32[4,512,8,128]{3,2,1,0:T(8,128)} copy(f32[4,512,8,128]{1,3,2,0:T(8,128)} %slice.29) | data formatting | bytes 16777216 | tf_op jit(solution)/shard_map/while/body/eval_jaxpr/slice | solution.py:83
  396.8 6.3 %reshape.80 = f32[16,131072]{1,0:T(8,128)} reshape(f32[4,512,8,128]{3,2,1,0:T(8,128)} %copy.45) | data formatting | bytes 16777216 | tf_op jit(solution)/shard_map/while/body/eval_jaxpr/reshape | solution.py:83
  403.0 6.0 convolution_convert_fusion
  412.5 15.9 %convert_bitcast_fusion = bf16[8192,1024]{0,1:T(8,128)(2,1)} fusion(bf16[512,8192]{1,0:T(8,128)(2,1)} %all-gather.7.cloned.1.call-done, bf16[64,8,8,128]{3,2,1,0:T(8,128)(2,1)S(1)} %bitcast.103), kind=kOutput, calls=%fused_computation.5 | convolution fusion | flops 8598323200 | bytes 26214400 | tf_op jit(solution)/shard_map/dot_general | solution.py:126
  431.9 5.9 fusion.8
  448.6 166.4 %reduce-scatter.8.cloned.1.call-done = bf16[1024,1024]{0,1:T(8,128)(2,1)} async-done(((bf16[8192,1024]{0,1:T(8,128)(2,1)}), bf16[1024,1024]{0,1:T(8,128)(2,1)}) %reduce-scatter.8.cloned.1.call-update) | async-done | bytes 2097168 | tf_op jit(solution)/shard_map/reduce_scatter | solution.py:125
  615.0 3.9 copy.47
  (69 shorter events, 58.8 us)
Async XLA Ops:
  7.2 4.4 copy-start.9
  7.2 5.6 copy-start.10
  7.2 34.3 %all-gather.5.cloned.1.call-start = ((), (), s32[]{:S(2)}) async-start(), calls=%async_computation.3 | async-start | bytes 2359296 | tf_op jit(solution)/shard_map/all_gather | solution.py:29
  7.9 63.8 %all-gather.11.cloned.1.call-start = ((), (), s32[]{:S(2)}) async-start(), calls=%async_computation.6 | async-start | bytes 2359296 | tf_op jit(solution)/shard_map/all_gather | solution.py:30
  8.7 152.0 %all-gather.7.cloned.1.call-start = ((), (), s32[]{:S(2)}) async-start(), calls=%async_computation.4 | async-start | bytes 10485760 | tf_op jit(solution)/shard_map/all_gather | solution.py:20
  9.4 303.9 %all-gather.9.cloned.1.call-start = ((), (), s32[]{:S(2)}) async-start(), calls=%async_computation.5 | async-start | bytes 18874368 | tf_op jit(solution)/shard_map/all_gather | solution.py:24
  10.0 435.0 %reduce-scatter.4.cloned.1.call-start = ((), (), s32[]{:S(2)}) async-start(), calls=%async_computation.7 | async-start | bytes 2359296 | tf_op jit(solution)/shard_map/reduce_scatter | solution.py:111
  83.1 3.9 copy-start.8
  83.1 4.4 copy-start.4
  87.0 3.8 copy-start.7
  87.4 4.6 copy-start.1
  108.5 4.0 copy-start.5
  343.5 2.3 copy-start.3
  347.3 3.9 copy-start.2
  374.1 72.7 %reduce-scatter.6.cloned.1.call-start = ((), (), s32[]{:S(2)}) async-start(), calls=%async_computation.8 | async-start | bytes 2359296 | tf_op jit(solution)/shard_map/reduce_scatter | solution.py:117
  378.6 3.9 copy-start
  409.1 2.4 copy-start.6
  411.4 203.5 %reduce-scatter.8.cloned.1.call-start = ((), (), s32[]{:S(2)}) async-start(), calls=%async_computation.9 | async-start | bytes 18874368 | tf_op jit(solution)/shard_map/reduce_scatter | solution.py:125
Sparse Core Ops, SparseCore 0:
  9.6 31.7 all-gather.4
  43.1 28.5 all-gather.10
  73.5 87.0 all-gather.6
  162.1 151.0 all-gather.8
  374.2 33.9 reduce-scatter.3
  411.5 33.9 reduce-scatter.5
  447.9 166.9 reduce-scatter.7
where the time goes:
time: 631 us; the launch traced here: 626 us
  waiting for transfers between devices  420 us (67%)
  local copies, waits for them, and re-layouts  97.8 us (15%)
  matrix products  74.2 us (12%)
  other arithmetic  19.3 us (3%)
  between operations  14.7 us (2%)
    reduce_scatter x1, waiting for transfers between devices, per_device(): lax.psum_scatter(lax.dot_general(columns, attn_out, (((0,), (0,)), ((), (...  166 us
    all_gather x1, waiting for transfers between devices, per_device(): lax.all_gather(proj_weight, 'col', axis=0, tiled=True)  153 us
    all_gather x1, waiting for transfers between devices, per_device(): full_grads = lax.all_gather(grad_out, 'row', axis=1, tiled=True)  44.4 us
    unnamed x32, local copies, waits for them, and re-layouts  36.8 us
    all_gather x1, waiting for transfers between devices, per_device(): lax.all_gather(cache_values, 'col', axis=0, tiled=True)  28 us
    all_gather x1, waiting for transfers between devices, per_device(): lax.all_gather(cache_keys, 'col', axis=0, tiled=True)  25.8 us
    dot_general x1, matrix products, per_device(): lax.dot_general(columns, attn_out, (((0,), (0,)), ((), ())), preferred_el...  15.9 us
    dot_general x1, matrix products, per_device(): jnp.dot(columns, lax.all_gather(proj_weight, 'col', axis=0, tiled=True),...  14.8 us
  transfers between devices with their start and end apart: 7, of which 5 were waited for; matrix products, arithmetic and copies ran while one was open for 19% of the time, Pallas kernels for 0%

commit v1 on v0

--- a/solution.py
+++ b/solution.py
@@ -3,6 +3,8 @@
 import jax
 import jax.numpy as jnp
 from jax import lax
+from jax.experimental import pallas as pl
+from jax.experimental.pallas import tpu as pltpu
 from jax.sharding import PartitionSpec as P
 
 HEAD_DIM = 128
@@ -133,6 +135,415 @@
     return (grad_q, grad_k, grad_v, grad_cache_k, grad_cache_v, grad_weight)
 
 
+F32 = jnp.float32
+BF16 = jnp.bfloat16
+INV = 1.0 / math.sqrt(HEAD_DIM)
+NZ = 4
+NEG = -1e30
+
+
+def dot_nt(a, b):
+    return lax.dot_general(a, b, (((1,), (1,)), ((), ())), preferred_element_type=F32)
+
+
+def dot_tn(a, b):
+    return lax.dot_general(a, b, (((0,), (0,)), ((), ())), preferred_element_type=F32)
+
+
+def dot_nn(a, b):
+    return jnp.dot(a, b, preferred_element_type=F32)
+
+
+def fused_kernel(
+    go, w, cache, q, k, v, bias,
+    gq, gk, gv, gc, gw,
+    G, wbuf, ckv, abuf, gacc, grecv, ga, rbuf, cpart, crecv, cbuf, pscr, dscr,
+    loc_sem, c_up, c_dn, c_rv, c_ps, c_pr, g_s, g_r, w_up, w_dn, w_rv, x_s, x_r,
+    r_up, r_dn, r_rv, s_up, s_dn, s_rv,
+):
+    col = lax.axis_index("col")
+    row = lax.axis_index("row")
+    z = col // 2
+    core = col % 2
+    other = 1 - core
+    has_up = z < NZ - 1
+    has_dn = z > 0
+    partner = {"col": z * 2 + other}
+    up = {"col": jnp.minimum(col + 2, 2 * NZ - 2 + core)}
+    dn = {"col": jnp.maximum(col - 2, core)}
+    rx = row + 1 - 2 * (row % 2)
+    ry = (row + 2) % 4
+    rd = (rx + 2) % 4
+    xn = {"row": rx}
+    yn = {"row": ry}
+    tok = q.shape[0]
+    wid = q.shape[1]
+    half = wid // 2
+    dblk = w.shape[0]
+    pending = []
+
+    def rcopy(src, dst, ss, rs, dev):
+        return pltpu.make_async_remote_copy(
+            src_ref=src, dst_ref=dst, send_sem=ss, recv_sem=rs,
+            device_id=dev, device_id_type=pl.DeviceIdType.MESH,
+        )
+
+    def when(cond, fn):
+        if cond is None:
+            fn()
+        else:
+            pl.when(cond)(fn)
+
+    def send(copy, cond=None):
+        when(cond, copy.start)
+        pending.append((copy, cond))
+
+    def arrived(ref, sem, cond=None):
+        when(cond, lambda: pltpu.make_async_copy(ref, ref, sem).wait())
+
+    barrier = pltpu.get_barrier_semaphore()
+
+    def greet(dev):
+        pl.semaphore_signal(barrier, inc=1, device_id=dev, device_id_type=pl.DeviceIdType.MESH)
+
+    for dev in (partner, xn, yn):
+        greet(dev)
+    pl.when(has_up)(lambda: greet(up))
+    pl.when(has_dn)(lambda: greet(dn))
+    pl.semaphore_wait(barrier, 3 + jnp.where(has_up, 1, 0) + jnp.where(has_dn, 1, 0))
+
+    send(rcopy(cache, ckv.at[z, core], c_up.at[0], c_rv.at[z], up), has_up)
+    send(rcopy(cache, ckv.at[z, core], c_dn.at[0], c_rv.at[z], dn), has_dn)
+    send(rcopy(cache, ckv.at[z, core], c_ps.at[0], c_pr.at[z], partner))
+    mine = pl.ds(pl.multiple_of(core * dblk, dblk), dblk)
+    theirs = pl.ds(pl.multiple_of(other * dblk, dblk), dblk)
+    trow = pl.ds(pl.multiple_of(core * tok, tok), tok)
+    orow = pl.ds(pl.multiple_of(other * tok, tok), tok)
+    send(rcopy(go.at[:, theirs], G.at[row, trow], g_s.at[0], g_r.at[0], partner))
+    send(rcopy(go.at[:, mine], G.at[row, trow], g_s.at[1], g_r.at[1 + core], xn))
+    send(rcopy(go.at[:, mine], G.at[row, trow], g_s.at[2], g_r.at[3 + core], yn))
+
+    locals_ = [
+        pltpu.make_async_copy(cache, ckv.at[z, core], loc_sem.at[0]),
+        pltpu.make_async_copy(go.at[:, mine], G.at[row, trow], loc_sem.at[1]),
+        pltpu.make_async_copy(w.at[:, pl.ds(0, half)], wbuf.at[z, 0], loc_sem.at[2]),
+        pltpu.make_async_copy(w.at[:, pl.ds(half, half)], wbuf.at[z, 1], loc_sem.at[3]),
+    ]
+    for c in locals_:
+        c.start()
+
+    def cache_step(t):
+        below, above = z - t, z + t
+        lo, hi = jnp.maximum(below, 0), jnp.minimum(above, NZ - 1)
+        got_lo, got_hi = below >= 0, above < NZ
+        arrived(ckv.at[lo, core], c_rv.at[lo], got_lo)
+        if t < NZ - 1:
+            send(rcopy(ckv.at[lo, core], ckv.at[lo, core], c_up.at[t], c_rv.at[lo], up),
+                 jnp.logical_and(got_lo, has_up))
+        send(rcopy(ckv.at[lo, core], ckv.at[lo, core], c_ps.at[2 * t - 1], c_pr.at[lo], partner), got_lo)
+        arrived(ckv.at[hi, core], c_rv.at[hi], got_hi)
+        if t < NZ - 1:
+            send(rcopy(ckv.at[hi, core], ckv.at[hi, core], c_dn.at[t], c_rv.at[hi], dn),
+                 jnp.logical_and(got_hi, has_dn))
+        send(rcopy(ckv.at[hi, core], ckv.at[hi, core], c_ps.at[2 * t], c_pr.at[hi], partner), got_hi)
+
+    def w_own(h):
+        src = w.at[:, pl.ds(h * half, half)]
+        send(rcopy(src, wbuf.at[z, h], w_up.at[0, h], w_rv.at[z, h], up), has_up)
+        send(rcopy(src, wbuf.at[z, h], w_dn.at[0, h], w_rv.at[z, h], dn), has_dn)
+
+    def w_step(t, h):
+        below, above = z - t, z + t
+        lo, hi = jnp.maximum(below, 0), jnp.minimum(above, NZ - 1)
+        got_lo, got_hi = below >= 0, above < NZ
+        arrived(wbuf.at[lo, h], w_rv.at[lo, h], got_lo)
+        if t < NZ - 1:
+            send(rcopy(wbuf.at[lo, h], wbuf.at[lo, h], w_up.at[t, h], w_rv.at[lo, h], up),
+                 jnp.logical_and(got_lo, has_up))
+        arrived(wbuf.at[hi, h], w_rv.at[hi, h], got_hi)
+        if t < NZ - 1:
+            send(rcopy(wbuf.at[hi, h], wbuf.at[hi, h], w_dn.at[t, h], w_rv.at[hi, h], dn),
+                 jnp.logical_and(got_hi, has_dn))
+
+    def clear(s):
+        rbuf[s] = jnp.zeros(rbuf.shape[1:], BF16)
+        for h in range(2):
+            cbuf[h, s] = jnp.zeros(cbuf.shape[2:], BF16)
+
+    @pl.when(z == 0)
+    def _():
+        lax.fori_loop(0, NZ, lambda s, c: (clear(s), c)[1], 0)
+
+    @pl.when(z == NZ - 1)
+    def _():
+        lax.fori_loop(0, NZ - 1, lambda s, c: (clear(s), c)[1], 0)
+        clear(NZ)
+
+    cache_step(1)
+    w_own(0)
+    arrived(G.at[row, orow], g_r.at[0])
+    send(rcopy(G.at[row, orow], G.at[row, orow], g_s.at[3], g_r.at[1 + other], xn))
+    send(rcopy(G.at[row, orow], G.at[row, orow], g_s.at[4], g_r.at[3 + other], yn))
+    cache_step(2)
+    cache_step(3)
+    for c in locals_:
+        c.wait()
+    for s in range(NZ):
+        arrived(ckv.at[s, other], c_pr.at[s])
+
+    causal = (lax.broadcasted_iota(jnp.int32, (BLOCK, BLOCK), 0)
+              >= lax.broadcasted_iota(jnp.int32, (BLOCK, BLOCK), 1))
+    blocks = tok // BLOCK
+
+    def head_cols(h):
+        return pl.ds(pl.multiple_of(h * HEAD_DIM, HEAD_DIM), HEAD_DIM)
+
+    def cached(kv, cols):
+        return ckv[:, :, kv, :, cols].reshape(CACHE, HEAD_DIM)
+
+    def probs_of(b, cols, kc):
+        rows = pl.ds(b * BLOCK, BLOCK)
+        qb = q[rows, cols]
+        s1 = dot_nt(qb, kc) * INV + bias[b]
+        s2 = jnp.where(causal, dot_nt(qb, k[rows, cols]) * INV, NEG)
+        m = jnp.maximum(jnp.max(s1, axis=1, keepdims=True), jnp.max(s2, axis=1, keepdims=True))
+        e1 = jnp.exp(s1 - m)
+        e2 = jnp.exp(s2 - m)
+        r = 1.0 / (jnp.sum(e1, axis=1, keepdims=True) + jnp.sum(e2, axis=1, keepdims=True))
+        return e1 * r, e2 * r
+
+    def fwd_head(h, c):
+        cols = head_cols(h)
+        kc = cached(0, cols)
+        vc = cached(1, cols)
+        for b in range(blocks):
+            rows = pl.ds(b * BLOCK, BLOCK)
+            p1, p2 = probs_of(b, cols, kc)
+            o = dot_nn(p1.astype(BF16), vc) + dot_nn(p2.astype(BF16), v[rows, cols])
+            abuf[pl.ds(pl.multiple_of(core * tok + b * BLOCK, BLOCK), BLOCK), cols] = o.astype(BF16)
+        return c
+
+    lax.fori_loop(0, wid // HEAD_DIM, fwd_head, 0)
+    send(rcopy(abuf.at[trow], abuf.at[trow], x_s.at[0], x_r.at[0], partner))
+
+    w_step(1, 0)
+    w_own(1)
+
+    first, second = pl.ds(0, tok), pl.ds(tok, tok)
+    arrived(G.at[rx, first], g_r.at[1])
+    send(rcopy(G.at[rx, first], G.at[rx, first], g_s.at[5], g_r.at[5], yn))
+    arrived(G.at[ry, second], g_r.at[4])
+    send(rcopy(G.at[ry, second], G.at[ry, second], g_s.at[6], g_r.at[6], xn))
+    arrived(G.at[rx, second], g_r.at[2])
+    arrived(G.at[ry, first], g_r.at[3])
+    w_step(2, 0)
+    arrived(G.at[rd, first], g_r.at[5])
+    arrived(G.at[rd, second], g_r.at[6])
+    arrived(abuf.at[orow], x_r.at[0])
+
+    tile = 256
+
+    def wg_tile(zd, h, n):
+        rows = pl.ds(pl.multiple_of(n * tile, tile), tile)
+        return rows, dot_tn(G[zd, :, rows], abuf[:, pl.ds(h * half, half)])
+
+    def rs_step(t, h):
+        zu = NZ - 1 - t + z
+        go_up = jnp.logical_and(zu > z, zu < NZ)
+        su = jnp.clip(zu, 0, NZ - 1)
+        zl = t - (NZ - 1) + z
+        go_dn = jnp.logical_and(zl >= 0, zl < z)
+        sl = jnp.clip(zl, 0, NZ - 1)
+        for go_, s, got, sems, dev, dst in (
+            (go_up, su, has_dn, r_up, up, su),
+            (go_dn, sl, has_up, r_dn, dn, jnp.where(zl == z - 1, NZ, sl)),
+        ):
+            arrived(rbuf.at[s, h], r_rv.at[s, h], jnp.logical_and(go_, got))
+
+            @pl.when(go_)
+            def _(s=s):
+                def body(n, c):
+                    rows, part = wg_tile(s, h, n)
+                    rbuf[s, h, rows, :] = (rbuf[s, h, rows, :].astype(F32) + part).astype(BF16)
+                    return c
+                lax.fori_loop(0, dblk // tile, body, 0)
+
+            send(rcopy(rbuf.at[s, h], rbuf.at[dst, h], sems.at[t, h], r_rv.at[dst, h], dev), go_)
+
+    def ga_part(h):
+        def body(n, c):
+            rows = pl.ds(pl.multiple_of(n * tile, tile), tile)
+            acc = dot_nn(G[0, rows, :], wbuf[0, h])
+            for s in range(1, NZ):
+                acc = acc + dot_nn(G[s, rows, :], wbuf[s, h])
+            gacc[h, rows, :] = acc
+            return c
+        lax.fori_loop(0, 2 * tok // tile, body, 0)
+        send(rcopy(gacc.at[h, orow], grecv.at[h], x_s.at[1 + h], x_r.at[1 + h], partner))
+
+    def bwd(h):
+        arrived(grecv.at[h], x_r.at[1 + h])
+        ga[...] = (gacc[h, trow, :] + grecv[h]).astype(BF16)
+
+        def head(j, c):
+            cols = head_cols(h * (half // HEAD_DIM) + j)
+            jc = head_cols(j)
+            kc = cached(0, cols)
+            vc = cached(1, cols)
+            for b in range(blocks):
+                rows = pl.ds(b * BLOCK, BLOCK)
+                p1, p2 = probs_of(b, cols, kc)
+                gb = ga[rows, jc]
+                d1 = dot_nt(gb, vc)
+                d2 = dot_nt(gb, v[rows, cols])
+                b1 = p1.astype(BF16)
+                b2 = p2.astype(BF16)
+                delta = (jnp.sum(b1.astype(F32) * d1, axis=1, keepdims=True)
+                         + jnp.sum(b2.astype(F32) * d2, axis=1, keepdims=True))
+                t1 = (p1 * (d1 - delta)).astype(BF16)
+                t2 = (p2 * (d2 - delta)).astype(BF16)
+                pscr[rows, :] = b1
+                dscr[rows, :] = t1
+                kb = k[rows, cols]
+                gq[rows, cols] = ((dot_nn(t1, kc) + dot_nn(t2, kb)) * INV).astype(BF16)
+                gk[rows, cols] = (dot_tn(t2, q[rows, cols]) * INV).astype(BF16)
+                gv[rows, cols] = dot_tn(b2, gb).astype(BF16)
+            ck = (dot_tn(dscr[...], q[:, cols]) * INV).astype(BF16)
+            cv = dot_tn(pscr[...], ga[:, jc]).astype(BF16)
+            for kv, part in ((0, ck), (1, cv)):
+                part = part.reshape(NZ, 2, BLOCK, HEAD_DIM)
+                for s in range(NZ):
+                    for side in range(2):
+                        cpart[h, side, s, kv, :, jc] = part[s, side]
+            return c
+
+        lax.fori_loop(0, half // HEAD_DIM, head, 0)
+        send(rcopy(cpart.at[h, other], crecv.at[h], x_s.at[3 + h], x_r.at[3 + h], partner))
+
+    def pair_sum(h):
+        arrived(crecv.at[h], x_r.at[3 + h])
+
+    def cache_sum(h, s):
+        return cpart[h, core, s].astype(F32) + crecv[h, s].astype(F32)
+
+    def crs_step(t, h):
+        zu = NZ - 1 - t + z
+        go_up = jnp.logical_and(zu > z, zu < NZ)
+        su = jnp.clip(zu, 0, NZ - 1)
+        zl = t - (NZ - 1) + z
+        go_dn = jnp.logical_and(zl >= 0, zl < z)
+        sl = jnp.clip(zl, 0, NZ - 1)
+        for go_, s, got, sems, dev, dst in (
+            (go_up, su, has_dn, s_up, up, su),
+            (go_dn, sl, has_up, s_dn, dn, jnp.where(zl == z - 1, NZ, sl)),
+        ):
+            arrived(cbuf.at[h, s], s_rv.at[s, h], jnp.logical_and(go_, got))
+
+            @pl.when(go_)
+            def _(s=s):
+                cbuf[h, s] = (cbuf[h, s].astype(F32) + cache_sum(h, s)).astype(BF16)
+
+            send(rcopy(cbuf.at[h, s], cbuf.at[h, dst], sems.at[t, h], s_rv.at[dst, h], dev), go_)
+
+    rs_step(0, 0)
+    rs_step(0, 1)
+    w_step(3, 0)
+    ga_part(0)
+    w_step(1, 1)
+    rs_step(1, 0)
+    bwd(0)
+    w_step(2, 1)
+    rs_step(1, 1)
+    pair_sum(0)
+    crs_step(0, 0)
+    rs_step(2, 0)
+    crs_step(1, 0)
+    rs_step(2, 1)
+    w_step(3, 1)
+    ga_part(1)
+    crs_step(2, 0)
+    bwd(1)
+    pair_sum(1)
+    for t in range(NZ - 1):
+        crs_step(t, 1)
+
+    for h in range(2):
+        arrived(rbuf.at[z, h], r_rv.at[z, h], has_dn)
+        arrived(rbuf.at[NZ, h], r_rv.at[NZ, h], has_up)
+
+        def last(n, c, h=h):
+            rows, part = wg_tile(z, h, n)
+            total = part + rbuf[z, h, rows, :].astype(F32) + rbuf[NZ, h, rows, :].astype(F32)
+            gw[rows, pl.ds(h * half, half)] = total.astype(BF16)
+            return c
+
+        lax.fori_loop(0, dblk // tile, last, 0)
+    for h in range(2):
+        arrived(cbuf.at[h, z], s_rv.at[z, h], has_dn)
+        arrived(cbuf.at[h, NZ], s_rv.at[NZ, h], has_up)
+        gc[:, :, pl.ds(h * half, half)] = (
+            cache_sum(h, z) + cbuf[h, z].astype(F32) + cbuf[h, NZ].astype(F32)
+        )
+
+    for copy, cond in pending:
+        when(cond, copy.wait_send)
+
+
+def per_device_fused(grad_out, proj_weight, queries, keys, values, cache_keys, cache_values, block_table):
+    tok, wid = queries.shape
+    half = wid // 2
+    dblk = proj_weight.shape[0]
+    blocks = tok // BLOCK
+    cache = jnp.stack([cache_keys, cache_values])
+    named = jnp.any(block_table[:, :, None] == jnp.arange(CB, dtype=jnp.int32), axis=1)
+    bias = jnp.repeat(jnp.where(named, 0.0, NEG).astype(F32), BLOCK, axis=1).reshape(blocks, 1, CACHE)
+    vm = pl.BlockSpec(memory_space=pltpu.VMEM)
+    hbm = pl.BlockSpec(memory_space=pl.ANY)
+    dma = pltpu.SemaphoreType.DMA
+    out = pl.pallas_call(
+        fused_kernel,
+        out_shape=(
+            jax.ShapeDtypeStruct((tok, wid), BF16),
+            jax.ShapeDtypeStruct((tok, wid), BF16),
+            jax.ShapeDtypeStruct((tok, wid), BF16),
+            jax.ShapeDtypeStruct((2, BLOCK, wid), F32),
+            jax.ShapeDtypeStruct((dblk, wid), BF16),
+        ),
+        in_specs=[hbm, hbm, hbm, vm, vm, vm, vm],
+        out_specs=[vm] * 5,
+        scratch_shapes=[
+            pltpu.VMEM((NZ, 2 * tok, dblk), BF16),
+            pltpu.VMEM((NZ, 2, dblk, half), BF16),
+            pltpu.VMEM((NZ, 2, 2, BLOCK, wid), BF16),
+            pltpu.VMEM((2 * tok, wid), BF16),
+            pltpu.VMEM((2, 2 * tok, half), F32),
+            pltpu.VMEM((2, tok, half), F32),
+            pltpu.VMEM((tok, half), BF16),
+            pltpu.VMEM((NZ + 1, 2, dblk, half), BF16),
+            pltpu.VMEM((2, 2, NZ, 2, BLOCK, half), BF16),
+            pltpu.VMEM((2, NZ, 2, BLOCK, half), BF16),
+            pltpu.VMEM((2, NZ + 1, 2, BLOCK, half), BF16),
+            pltpu.VMEM((tok, CACHE), BF16),
+            pltpu.VMEM((tok, CACHE), BF16),
+            dma((4,)), dma((3,)), dma((3,)), dma((NZ,)), dma((7,)), dma((NZ,)),
+            dma((7,)), dma((7,)),
+            dma((3, 2)), dma((3, 2)), dma((NZ, 2)),
+            dma((5,)), dma((5,)),
+            dma((3, 2)), dma((3, 2)), dma((NZ + 1, 2)),
+            dma((3, 2)), dma((3, 2)), dma((NZ + 1, 2)),
+        ],
+        compiler_params=pltpu.CompilerParams(
+            collective_id=0, has_side_effects=True, vmem_limit_bytes=64 * 1024 * 1024
+        ),
+        name="fused",
+    )(grad_out, proj_weight, cache, queries, keys, values, bias)
+    return out[0], out[1], out[2], out[3][0], out[3][1], out[4]
+
+
+def fits_fused(mesh):
+    return mesh.shape["row"] == 4 and mesh.shape["col"] == 2 * NZ
+
+
 def solution(mesh):
     in_specs = (
         P("col", "row"),
@@ -153,5 +564,5 @@
         P("col", "row"),
     )
     return jax.shard_map(
-        per_device, mesh=mesh, in_specs=in_specs, out_specs=out_specs, check_vma=False
-    )
+        per_device_fused if fits_fused(mesh) else per_device, mesh=mesh, in_specs=in_specs, out_specs=out_specs, check_vma=False
+    )

time: 631 us -> 300 us (0.48)
  waiting for transfers between devices: 420 us -> 0 us
  Pallas kernels: 0 us -> 289 us
  local copies, waits for them, and re-layouts: 97.8 us -> 7.5 us
  matrix products: 74.2 us -> 0 us
  other arithmetic: 19.3 us -> 2.65 us
  between operations: 14.7 us -> 0.66 us
    pallas_call x0 -> x1, Pallas kernels: none -> 289 us  [per_device_fused(): pl.pallas_call(fused_kernel, out_shape=(jax.ShapeDtypeStruct((tok, wid),...]
    all_gather x4 -> x0, waiting for transfers between devices: 251 us -> none  [the longest x1 153 us: per_device(): lax.all_gather(proj_weight, 'col', axis=0, tiled=True)]
    reduce_scatter x3 -> x0, waiting for transfers between devices: 166 us -> none  [the longest x1 166 us: per_device(): lax.psum_scatter(lax.dot_general(columns, attn_out, (((0,), (0,)), ((), (...]
    dot_general x10 -> x0, matrix products: 74.2 us -> none  [the longest x1 15.9 us: per_device(): lax.dot_general(columns, attn_out, (((0,), (0,)), ((), ())), preferred_el...]
    unnamed x32 -> x12, local copies, waits for them, and re-layouts: 36.8 us -> 4.39 us
    slice x8 -> x0, local copies, waits for them, and re-layouts: 28.3 us -> none  [the longest x2 14.3 us: one_group(): grad_value_list[:, :KB * BLOCK].reshape(group * KB, BLOCK * local_width)]
    reshape x3 -> x0, local copies, waits for them, and re-layouts: 14.4 us -> none  [the longest x1 6.27 us: one_group(): grad_value_list[:, :KB * BLOCK].reshape(group * KB, BLOCK * local_width)]
    sub x1 -> x0, other arithmetic: 11.1 us -> none  [one_group(): weights = jnp.exp(scores - row_max)]
  transfers between devices with their start and end apart: 7 -> 0, of which waited for: 5 -> 0; matrix products, arithmetic and copies ran while one was open for 19% -> 0% of each run, Pallas kernels for 0% -> 0%
where the time goes in v1:
time: 300 us; the launch traced here: 299 us
  Pallas kernels  289 us (96%)
  local copies, waits for them, and re-layouts  7.5 us (2%)
    pallas_call x1, Pallas kernels, per_device_fused(): pl.pallas_call(fused_kernel, out_shape=(jax.ShapeDtypeStruct((tok, wid),...  289 us

profile of v1, /device:TPU:0, one launch (start us, length us, event | category | flops | bytes accessed | tf_op | source)
XLA Modules:
  0.0 299.4 jit_solution(13559908492676969995)
XLA Ops:
  0.6 0.8 fusion
  1.4 0.7 broadcast_in_dim.15
  2.1 1.9 pad_maximum_fusion.cache
  4.0 288.6 %fused.1 = (bf16[512,1024]{1,0:T(8,128)(2,1)}, bf16[512,1024]{1,0:T(8,128)(2,1)}, bf16[512,1024]{1,0:T(8,128)(2,1)}, f32[2,128,1024]{2,1,0:T(8,128)}, bf16[1024,1024]{1,0:T(8,128)(2,1)}) custom-call(bf16[512,2048]{1,0:T(8,128)(2,1)} %go.1, bf16[1024,1024]{1,0:T(8,128)(2,1)} %w.1, bf16[2,128,1024]{2,1,0:T(8,128)(2,1)} %pad_maximum_fusion.cache, ...), custom_call_target="tpu_custom_call" | custom-call | tf_op jit(solution)/shard_map/fused/pallas_call | solution.py:503
  292.6 0.0 copy-start.3
  292.6 0.0 copy-start.2
  292.6 2.4 slice_bitcast_fusion
  295.0 0.0 copy-done.3
  295.0 0.0 copy-start.1
  295.0 1.0 copy.18
  296.0 0.0 copy-done.2
  296.0 0.0 copy-start
  296.0 1.0 copy.19
  297.0 0.0 copy-done.1
  297.0 1.0 copy.20
  298.0 0.1 copy-done
  298.1 1.3 copy.21
  (1 shorter events, 0.0 us)
Async XLA Ops:
  292.6 2.4 copy-start.3
  292.6 3.4 %copy-start.2 = (bf16[512,1024]{1,0:T(8,128)(2,1)S(1)}, bf16[512,1024]{1,0:T(8,128)(2,1)}, u32[]{:S(2)}) copy-start(bf16[512,1024]{1,0:T(8,128)(2,1)} %get-tuple-element.25) | copy-start | bytes 3145732
  295.0 1.9 copy-start.1
  296.0 2.1 copy-start

commit v2 on v1

--- a/solution.py
+++ b/solution.py
@@ -156,10 +156,10 @@
 
 def fused_kernel(
     go, w, cache, q, k, v, bias,
-    gq, gk, gv, gc, gw,
-    G, wbuf, ckv, abuf, gacc, grecv, ga, rbuf, cpart, crecv, cbuf, pscr, dscr,
-    loc_sem, c_up, c_dn, c_rv, c_ps, c_pr, g_s, g_r, w_up, w_dn, w_rv, x_s, x_r,
-    r_up, r_dn, r_rv, s_up, s_dn, s_rv,
+    gq, gk, gv, gc, gw, H, gx,
+    G, ckv, abuf, gpart, grecv, ga, rbuf, cpart, crecv, cbuf, pscr, dscr,
+    loc_sem, c_up, c_dn, c_rv, c_ps, c_pr, a_up, a_dn, a_rv, a_ps, a_pr,
+    g_s, g_r, p_s, p_r, x_s, x_r, r_up, r_dn, r_rv, s_up, s_dn, s_rv,
 ):
     col = lax.axis_index("col")
     row = lax.axis_index("row")
@@ -176,6 +176,7 @@
     rd = (rx + 2) % 4
     xn = {"row": rx}
     yn = {"row": ry}
+    dg = {"row": rd}
     tok = q.shape[0]
     wid = q.shape[1]
     half = wid // 2
@@ -206,64 +207,54 @@
     def greet(dev):
         pl.semaphore_signal(barrier, inc=1, device_id=dev, device_id_type=pl.DeviceIdType.MESH)
 
-    for dev in (partner, xn, yn):
+    zs_of = [(z + NZ - i) % NZ for i in range(NZ)]
+    zd_of = [(z + i) % NZ for i in range(NZ)]
+    line = [{"col": zd_of[i] * 2 + core} for i in range(NZ)]
+    for dev in (partner, xn, yn, dg, line[1], line[2], line[3]):
         greet(dev)
-    pl.when(has_up)(lambda: greet(up))
-    pl.when(has_dn)(lambda: greet(dn))
-    pl.semaphore_wait(barrier, 3 + jnp.where(has_up, 1, 0) + jnp.where(has_dn, 1, 0))
-
-    send(rcopy(cache, ckv.at[z, core], c_up.at[0], c_rv.at[z], up), has_up)
-    send(rcopy(cache, ckv.at[z, core], c_dn.at[0], c_rv.at[z], dn), has_dn)
-    send(rcopy(cache, ckv.at[z, core], c_ps.at[0], c_pr.at[z], partner))
+    pl.semaphore_wait(barrier, 7)
+
+    def line_own(src, buf, sems):
+        s_u, s_d, rv, ps, pr = sems
+        send(rcopy(src, buf.at[z, core], s_u.at[0], rv.at[z], up), has_up)
+        send(rcopy(src, buf.at[z, core], s_d.at[0], rv.at[z], dn), has_dn)
+        send(rcopy(src, buf.at[z, core], ps.at[0], pr.at[z], partner))
+
+    def line_step(t, buf, sems):
+        s_u, s_d, rv, ps, pr = sems
+        below, above = z - t, z + t
+        lo, hi = jnp.maximum(below, 0), jnp.minimum(above, NZ - 1)
+        got_lo, got_hi = below >= 0, above < NZ
+        for s, got, hop, ss, dev, n in (
+            (lo, got_lo, has_up, s_u, up, 2 * t - 1),
+            (hi, got_hi, has_dn, s_d, dn, 2 * t),
+        ):
+            piece = buf.at[s, core]
+            arrived(piece, rv.at[s], got)
+            if t < NZ - 1:
+                send(rcopy(piece, piece, ss.at[t], rv.at[s], dev), jnp.logical_and(got, hop))
+            send(rcopy(piece, piece, ps.at[n], pr.at[s], partner), got)
+
+    c_sems = (c_up, c_dn, c_rv, c_ps, c_pr)
+    a_sems = (a_up, a_dn, a_rv, a_ps, a_pr)
+    line_own(cache, ckv, c_sems)
     mine = pl.ds(pl.multiple_of(core * dblk, dblk), dblk)
     theirs = pl.ds(pl.multiple_of(other * dblk, dblk), dblk)
-    trow = pl.ds(pl.multiple_of(core * tok, tok), tok)
-    orow = pl.ds(pl.multiple_of(other * tok, tok), tok)
-    send(rcopy(go.at[:, theirs], G.at[row, trow], g_s.at[0], g_r.at[0], partner))
-    send(rcopy(go.at[:, mine], G.at[row, trow], g_s.at[1], g_r.at[1 + core], xn))
-    send(rcopy(go.at[:, mine], G.at[row, trow], g_s.at[2], g_r.at[3 + core], yn))
+    send(rcopy(go.at[:, theirs], gx, g_s.at[0], g_r.at[0], partner))
+
+    def quarter(r):
+        return pl.ds(pl.multiple_of(r * BLOCK, BLOCK), BLOCK)
+
+    plane = ((rx, xn), (ry, yn), (rd, dg))
+    for n, (r, dev) in enumerate(plane):
+        send(rcopy(go.at[quarter(r), mine], H.at[row, core], g_s.at[1 + n], g_r.at[1 + 2 * n + core], dev))
 
     locals_ = [
         pltpu.make_async_copy(cache, ckv.at[z, core], loc_sem.at[0]),
-        pltpu.make_async_copy(go.at[:, mine], G.at[row, trow], loc_sem.at[1]),
-        pltpu.make_async_copy(w.at[:, pl.ds(0, half)], wbuf.at[z, 0], loc_sem.at[2]),
-        pltpu.make_async_copy(w.at[:, pl.ds(half, half)], wbuf.at[z, 1], loc_sem.at[3]),
+        pltpu.make_async_copy(go.at[quarter(row), mine], H.at[row, core], loc_sem.at[1]),
     ]
     for c in locals_:
         c.start()
-
-    def cache_step(t):
-        below, above = z - t, z + t
-        lo, hi = jnp.maximum(below, 0), jnp.minimum(above, NZ - 1)
-        got_lo, got_hi = below >= 0, above < NZ
-        arrived(ckv.at[lo, core], c_rv.at[lo], got_lo)
-        if t < NZ - 1:
-            send(rcopy(ckv.at[lo, core], ckv.at[lo, core], c_up.at[t], c_rv.at[lo], up),
-                 jnp.logical_and(got_lo, has_up))
-        send(rcopy(ckv.at[lo, core], ckv.at[lo, core], c_ps.at[2 * t - 1], c_pr.at[lo], partner), got_lo)
-        arrived(ckv.at[hi, core], c_rv.at[hi], got_hi)
-        if t < NZ - 1:
-            send(rcopy(ckv.at[hi, core], ckv.at[hi, core], c_dn.at[t], c_rv.at[hi], dn),
-                 jnp.logical_and(got_hi, has_dn))
-        send(rcopy(ckv.at[hi, core], ckv.at[hi, core], c_ps.at[2 * t], c_pr.at[hi], partner), got_hi)
-
-    def w_own(h):
-        src = w.at[:, pl.ds(h * half, half)]
-        send(rcopy(src, wbuf.at[z, h], w_up.at[0, h], w_rv.at[z, h], up), has_up)
-        send(rcopy(src, wbuf.at[z, h], w_dn.at[0, h], w_rv.at[z, h], dn), has_dn)
-
-    def w_step(t, h):
-        below, above = z - t, z + t
-        lo, hi = jnp.maximum(below, 0), jnp.minimum(above, NZ - 1)
-        got_lo, got_hi = below >= 0, above < NZ
-        arrived(wbuf.at[lo, h], w_rv.at[lo, h], got_lo)
-        if t < NZ - 1:
-            send(rcopy(wbuf.at[lo, h], wbuf.at[lo, h], w_up.at[t, h], w_rv.at[lo, h], up),
-                 jnp.logical_and(got_lo, has_up))
-        arrived(wbuf.at[hi, h], w_rv.at[hi, h], got_hi)
-        if t < NZ - 1:
-            send(rcopy(wbuf.at[hi, h], wbuf.at[hi, h], w_dn.at[t, h], w_rv.at[hi, h], dn),
-                 jnp.logical_and(got_hi, has_dn))
 
     def clear(s):
         rbuf[s] = jnp.zeros(rbuf.shape[1:], BF16)
@@ -279,15 +270,42 @@
         lax.fori_loop(0, NZ - 1, lambda s, c: (clear(s), c)[1], 0)
         clear(NZ)
 
-    cache_step(1)
-    w_own(0)
-    arrived(G.at[row, orow], g_r.at[0])
-    send(rcopy(G.at[row, orow], G.at[row, orow], g_s.at[3], g_r.at[1 + other], xn))
-    send(rcopy(G.at[row, orow], G.at[row, orow], g_s.at[4], g_r.at[3 + other], yn))
-    cache_step(2)
-    cache_step(3)
+    line_step(1, ckv, c_sems)
+    arrived(gx, g_r.at[0])
+    for n, (r, dev) in enumerate(plane):
+        send(rcopy(gx.at[quarter(r)], H.at[row, other], g_s.at[4 + n], g_r.at[1 + 2 * n + other], dev))
+    own_gx = pltpu.make_async_copy(gx.at[quarter(row)], H.at[row, other], loc_sem.at[2])
+    own_gx.start()
+    line_step(2, ckv, c_sems)
     for c in locals_:
         c.wait()
+    own_gx.wait()
+    for n, (r, dev) in enumerate(plane):
+        for side in range(2):
+            arrived(H.at[r, side], g_r.at[1 + 2 * n + side])
+    own_h = pltpu.make_async_copy(H.at[z], G.at[z, :, row], loc_sem.at[3])
+    own_h.start()
+    for i in range(1, NZ):
+        send(rcopy(H.at[zd_of[i]], G.at[z, :, row], g_s.at[6 + i], g_r.at[6 + i], line[i]))
+
+    def plane_send(i):
+        piece = G.at[zs_of[i], :, row]
+        if i == 0:
+            own_h.wait()
+        else:
+            arrived(piece, g_r.at[6 + i])
+        send(rcopy(piece, piece, g_s.at[10 + i], g_r.at[10 + i], xn))
+        send(rcopy(piece, piece, g_s.at[14 + i], g_r.at[14 + i], yn))
+
+    def plane_pass(i):
+        zs = zs_of[i]
+        arrived(G.at[zs, :, rx], g_r.at[10 + i])
+        send(rcopy(G.at[zs, 0, rx], G.at[zs, 0, rx], g_s.at[18 + i], g_r.at[18 + i], yn))
+        arrived(G.at[zs, :, ry], g_r.at[14 + i])
+        send(rcopy(G.at[zs, 1, ry], G.at[zs, 1, ry], g_s.at[22 + i], g_r.at[22 + i], xn))
+
+    plane_send(0)
+    line_step(3, ckv, c_sems)
     for s in range(NZ):
         arrived(ckv.at[s, other], c_pr.at[s])
 
@@ -320,32 +338,44 @@
             rows = pl.ds(b * BLOCK, BLOCK)
             p1, p2 = probs_of(b, cols, kc)
             o = dot_nn(p1.astype(BF16), vc) + dot_nn(p2.astype(BF16), v[rows, cols])
-            abuf[pl.ds(pl.multiple_of(core * tok + b * BLOCK, BLOCK), BLOCK), cols] = o.astype(BF16)
+            abuf[z, core, rows, cols] = o.astype(BF16)
         return c
 
     lax.fori_loop(0, wid // HEAD_DIM, fwd_head, 0)
-    send(rcopy(abuf.at[trow], abuf.at[trow], x_s.at[0], x_r.at[0], partner))
-
-    w_step(1, 0)
-    w_own(1)
-
-    first, second = pl.ds(0, tok), pl.ds(tok, tok)
-    arrived(G.at[rx, first], g_r.at[1])
-    send(rcopy(G.at[rx, first], G.at[rx, first], g_s.at[5], g_r.at[5], yn))
-    arrived(G.at[ry, second], g_r.at[4])
-    send(rcopy(G.at[ry, second], G.at[ry, second], g_s.at[6], g_r.at[6], xn))
-    arrived(G.at[rx, second], g_r.at[2])
-    arrived(G.at[ry, first], g_r.at[3])
-    w_step(2, 0)
-    arrived(G.at[rd, first], g_r.at[5])
-    arrived(G.at[rd, second], g_r.at[6])
-    arrived(abuf.at[orow], x_r.at[0])
+    line_own(abuf.at[z, core], abuf, a_sems)
 
     tile = 256
 
-    def wg_tile(zd, h, n):
-        rows = pl.ds(pl.multiple_of(n * tile, tile), tile)
-        return rows, dot_tn(G[zd, :, rows], abuf[:, pl.ds(h * half, half)])
+    def ga_part(i):
+        zs = zs_of[i]
+        arrived(G.at[zs, 0, rd], g_r.at[18 + i])
+        arrived(G.at[zs, 1, rd], g_r.at[22 + i])
+
+        def body(n, c):
+            side = n // 2
+            part = n % 2
+            rows = pl.ds(pl.multiple_of(part * tile, tile), tile)
+            lhs = G[zs, side, pl.ds(part * 2, 2)].reshape(tile, dblk)
+            for h in range(2):
+                acc = dot_nn(lhs, w[:, pl.ds(h * half, half)])
+                gpart[side, zs, h, rows, :] = acc.astype(BF16)
+            return c
+
+        lax.fori_loop(0, 4, body, 0)
+        send(rcopy(gpart.at[other, zs], grecv.at[zs], p_s.at[i], p_r.at[i], partner))
+
+    def gw_tile(n):
+        rows = pl.ds(n * tile, tile)
+        acc = None
+        for s in range(NZ):
+            lhs = G[s, :, :, :, rows].reshape(2 * tok, tile)
+            part = dot_tn(lhs, abuf[s].reshape(2 * tok, wid))
+            acc = part if acc is None else acc + part
+        gw[rows, :] = acc.astype(BF16)
+
+    def ga_sum(s, h, rows):
+        return (gpart[core, s, h, rows, :].astype(F32) + grecv[s, h, rows, :].astype(F32)
+                + rbuf[s, h, rows, :].astype(F32))
 
     def rs_step(t, h):
         zu = NZ - 1 - t + z
@@ -363,27 +393,23 @@
             @pl.when(go_)
             def _(s=s):
                 def body(n, c):
-                    rows, part = wg_tile(s, h, n)
-                    rbuf[s, h, rows, :] = (rbuf[s, h, rows, :].astype(F32) + part).astype(BF16)
+                    rows = pl.ds(pl.multiple_of(n * BLOCK, BLOCK), BLOCK)
+                    rbuf[s, h, rows, :] = ga_sum(s, h, rows).astype(BF16)
                     return c
-                lax.fori_loop(0, dblk // tile, body, 0)
+                lax.fori_loop(0, tok // BLOCK, body, 0)
 
             send(rcopy(rbuf.at[s, h], rbuf.at[dst, h], sems.at[t, h], r_rv.at[dst, h], dev), go_)
 
-    def ga_part(h):
-        def body(n, c):
-            rows = pl.ds(pl.multiple_of(n * tile, tile), tile)
-            acc = dot_nn(G[0, rows, :], wbuf[0, h])
-            for s in range(1, NZ):
-                acc = acc + dot_nn(G[s, rows, :], wbuf[s, h])
-            gacc[h, rows, :] = acc
+    def bwd(h):
+        arrived(rbuf.at[z, h], r_rv.at[z, h], has_dn)
+        arrived(rbuf.at[NZ, h], r_rv.at[NZ, h], has_up)
+
+        def total(n, c):
+            rows = pl.ds(pl.multiple_of(n * BLOCK, BLOCK), BLOCK)
+            ga[rows, :] = (ga_sum(z, h, rows) + rbuf[NZ, h, rows, :].astype(F32)).astype(BF16)
             return c
-        lax.fori_loop(0, 2 * tok // tile, body, 0)
-        send(rcopy(gacc.at[h, orow], grecv.at[h], x_s.at[1 + h], x_r.at[1 + h], partner))
-
-    def bwd(h):
-        arrived(grecv.at[h], x_r.at[1 + h])
-        ga[...] = (gacc[h, trow, :] + grecv[h]).astype(BF16)
+
+        lax.fori_loop(0, blocks, total, 0)
 
         def head(j, c):
             cols = head_cols(h * (half // HEAD_DIM) + j)
@@ -418,10 +444,10 @@
             return c
 
         lax.fori_loop(0, half // HEAD_DIM, head, 0)
-        send(rcopy(cpart.at[h, other], crecv.at[h], x_s.at[3 + h], x_r.at[3 + h], partner))
+        send(rcopy(cpart.at[h, other], crecv.at[h], x_s.at[h], x_r.at[h], partner))
 
     def pair_sum(h):
-        arrived(crecv.at[h], x_r.at[3 + h])
+        arrived(crecv.at[h], x_r.at[h])
 
     def cache_sum(h, s):
         return cpart[h, core, s].astype(F32) + crecv[h, s].astype(F32)
@@ -445,39 +471,45 @@
 
             send(rcopy(cbuf.at[h, s], cbuf.at[h, dst], sems.at[t, h], s_rv.at[dst, h], dev), go_)
 
+    plane_send(1)
+    plane_pass(0)
+    line_step(1, abuf, a_sems)
+    plane_send(2)
+    ga_part(0)
+    plane_pass(1)
+    plane_send(3)
+    ga_part(1)
+    plane_pass(2)
+    line_step(2, abuf, a_sems)
+    ga_part(2)
+    plane_pass(3)
+    ga_part(3)
+    for i in range(NZ):
+        arrived(grecv.at[zs_of[i]], p_r.at[i])
     rs_step(0, 0)
     rs_step(0, 1)
-    w_step(3, 0)
-    ga_part(0)
-    w_step(1, 1)
+    line_step(3, abuf, a_sems)
     rs_step(1, 0)
+    rs_step(1, 1)
+    for s in range(NZ):
+        arrived(abuf.at[s, other], a_pr.at[s])
+    gw_tile(0)
+    rs_step(2, 0)
+    gw_tile(1)
+    rs_step(2, 1)
     bwd(0)
-    w_step(2, 1)
-    rs_step(1, 1)
     pair_sum(0)
     crs_step(0, 0)
-    rs_step(2, 0)
+    bwd(1)
     crs_step(1, 0)
-    rs_step(2, 1)
-    w_step(3, 1)
-    ga_part(1)
+    pair_sum(1)
+    crs_step(0, 1)
     crs_step(2, 0)
-    bwd(1)
-    pair_sum(1)
-    for t in range(NZ - 1):
-        crs_step(t, 1)
-
-    for h in range(2):
-        arrived(rbuf.at[z, h], r_rv.at[z, h], has_dn)
-        arrived(rbuf.at[NZ, h], r_rv.at[NZ, h], has_up)
-
-        def last(n, c, h=h):
-            rows, part = wg_tile(z, h, n)
-            total = part + rbuf[z, h, rows, :].astype(F32) + rbuf[NZ, h, rows, :].astype(F32)
-            gw[rows, pl.ds(h * half, half)] = total.astype(BF16)
-            return c
-
-        lax.fori_loop(0, dblk // tile, last, 0)
+    gw_tile(2)
+    crs_step(1, 1)
+    gw_tile(3)
+    crs_step(2, 1)
+
     for h in range(2):
         arrived(cbuf.at[h, z], s_rv.at[z, h], has_dn)
         arrived(cbuf.at[h, NZ], s_rv.at[NZ, h], has_up)
@@ -508,27 +540,30 @@
             jax.ShapeDtypeStruct((tok, wid), BF16),
             jax.ShapeDtypeStruct((2, BLOCK, wid), F32),
             jax.ShapeDtypeStruct((dblk, wid), BF16),
+            jax.ShapeDtypeStruct((NZ, 2, BLOCK, dblk), BF16),
+            jax.ShapeDtypeStruct((tok, dblk), BF16),
         ),
-        in_specs=[hbm, hbm, hbm, vm, vm, vm, vm],
-        out_specs=[vm] * 5,
+        in_specs=[hbm, vm, hbm, vm, vm, vm, vm],
+        out_specs=[vm] * 5 + [hbm] * 2,
         scratch_shapes=[
-            pltpu.VMEM((NZ, 2 * tok, dblk), BF16),
-            pltpu.VMEM((NZ, 2, dblk, half), BF16),
+            pltpu.VMEM((NZ, 2, 4, BLOCK, dblk), BF16),
             pltpu.VMEM((NZ, 2, 2, BLOCK, wid), BF16),
-            pltpu.VMEM((2 * tok, wid), BF16),
-            pltpu.VMEM((2, 2 * tok, half), F32),
-            pltpu.VMEM((2, tok, half), F32),
+            pltpu.VMEM((NZ, 2, tok, wid), BF16),
+            pltpu.VMEM((2, NZ, 2, tok, half), BF16),
+            pltpu.VMEM((NZ, 2, tok, half), BF16),
             pltpu.VMEM((tok, half), BF16),
-            pltpu.VMEM((NZ + 1, 2, dblk, half), BF16),
+            pltpu.VMEM((NZ + 1, 2, tok, half), BF16),
             pltpu.VMEM((2, 2, NZ, 2, BLOCK, half), BF16),
             pltpu.VMEM((2, NZ, 2, BLOCK, half), BF16),
             pltpu.VMEM((2, NZ + 1, 2, BLOCK, half), BF16),
             pltpu.VMEM((tok, CACHE), BF16),
             pltpu.VMEM((tok, CACHE), BF16),
-            dma((4,)), dma((3,)), dma((3,)), dma((NZ,)), dma((7,)), dma((NZ,)),
-            dma((7,)), dma((7,)),
-            dma((3, 2)), dma((3, 2)), dma((NZ, 2)),
-            dma((5,)), dma((5,)),
+            dma((4,)),
+            dma((3,)), dma((3,)), dma((NZ,)), dma((7,)), dma((NZ,)),
+            dma((3,)), dma((3,)), dma((NZ,)), dma((7,)), dma((NZ,)),
+            dma((26,)), dma((26,)),
+            dma((NZ,)), dma((NZ,)),
+            dma((2,)), dma((2,)),
             dma((3, 2)), dma((3, 2)), dma((NZ + 1, 2)),
             dma((3, 2)), dma((3, 2)), dma((NZ + 1, 2)),
         ],

time: 300 us -> 284 us (0.947)
  Pallas kernels: 289 us -> 272 us
    pallas_call x1, Pallas kernels: 289 us -> 272 us  [per_device_fused(): pl.pallas_call(fused_kernel, out_shape=(jax.ShapeDtypeStruct((tok, wid),...]
where the time goes in v2:
time: 284 us; the launch traced here: 283 us
  Pallas kernels  272 us (96%)
  local copies, waits for them, and re-layouts  7.5 us (3%)
    pallas_call x1, Pallas kernels, per_device_fused(): pl.pallas_call(fused_kernel, out_shape=(jax.ShapeDtypeStruct((tok, wid),...  272 us

profile of v2, /device:TPU:0, one launch (start us, length us, event | category | flops | bytes accessed | tf_op | source)
XLA Modules:
  0.0 282.9 jit_solution(9640281066733750839)
XLA Ops:
  0.6 0.8 fusion
  1.4 0.7 broadcast_in_dim.15
  2.1 1.9 pad_maximum_fusion.cache
  4.0 272.1 %fused.1 = (bf16[512,1024]{1,0:T(8,128)(2,1)}, bf16[512,1024]{1,0:T(8,128)(2,1)}, bf16[512,1024]{1,0:T(8,128)(2,1)}, f32[2,128,1024]{2,1,0:T(8,128)}, bf16[1024,...) custom-call(bf16[512,2048]{1,0:T(8,128)(2,1)} %go.1, bf16[1024,1024]{1,0:T(8,128)(2,1)} %w.1, ...), custom_call_target="tpu_custom_call" | custom-call | tf_op jit(solution)/shard_map/fused/pallas_call | solution.py:535
  276.0 0.0 copy-start.3
  276.0 0.0 copy-start.2
  276.0 2.4 slice_bitcast_fusion
  278.5 0.0 copy-done.3
  278.5 0.0 copy-start.1
  278.5 1.0 copy.18
  279.4 0.0 copy-done.2
  279.5 0.0 copy-start
  279.5 1.0 copy.19
  280.4 0.0 copy-done.1
  280.4 1.0 copy.20
  281.4 0.1 copy-done
  281.5 1.3 copy.21
  (1 shorter events, 0.0 us)
Async XLA Ops:
  276.0 2.4 copy-start.3
  276.0 3.4 %copy-start.2 = (bf16[512,1024]{1,0:T(8,128)(2,1)S(1)}, bf16[512,1024]{1,0:T(8,128)(2,1)}, u32[]{:S(2)}) copy-start(bf16[512,1024]{1,0:T(8,128)(2,1)} %get-tuple-element.25) | copy-start | bytes 3145732
  278.5 1.9 copy-start.1
  279.5 2.1 copy-start

commit v3 on v2

--- a/solution.py
+++ b/solution.py
@@ -140,6 +140,7 @@
 INV = 1.0 / math.sqrt(HEAD_DIM)
 NZ = 4
 NEG = -1e30
+INV2 = INV * math.log2(math.e)
 
 
 def dot_nt(a, b):
@@ -155,9 +156,9 @@
 
 
 def fused_kernel(
-    go, w, cache, q, k, v, bias,
-    gq, gk, gv, gc, gw, H, gx,
-    G, ckv, abuf, gpart, grecv, ga, rbuf, cpart, crecv, cbuf, pscr, dscr,
+    go, w, cache, q, k, v, tz, tc, slot_of,
+    gq, gk, gv, gck, gcv, gw, H, gx,
+    G, ckv, abuf, gpart, grecv, ga, rbuf, cpart, crecv, cbuf, pscr, dscr, lse,
     loc_sem, c_up, c_dn, c_rv, c_ps, c_pr, a_up, a_dn, a_rv, a_ps, a_pr,
     g_s, g_r, p_s, p_r, x_s, x_r, r_up, r_dn, r_rv, s_up, s_dn, s_rv,
 ):
@@ -316,31 +317,32 @@
     def head_cols(h):
         return pl.ds(pl.multiple_of(h * HEAD_DIM, HEAD_DIM), HEAD_DIM)
 
-    def cached(kv, cols):
-        return ckv[:, :, kv, :, cols].reshape(CACHE, HEAD_DIM)
-
-    def probs_of(b, cols, kc):
-        rows = pl.ds(b * BLOCK, BLOCK)
+    def listed(kv, b, cols):
+        return jnp.concatenate([ckv[tz[b, j], tc[b, j], kv, :, cols] for j in range(KB)], axis=0)
+
+    def scores_of(rows, cols, kc):
         qb = q[rows, cols]
-        s1 = dot_nt(qb, kc) * INV + bias[b]
-        s2 = jnp.where(causal, dot_nt(qb, k[rows, cols]) * INV, NEG)
-        m = jnp.maximum(jnp.max(s1, axis=1, keepdims=True), jnp.max(s2, axis=1, keepdims=True))
-        e1 = jnp.exp(s1 - m)
-        e2 = jnp.exp(s2 - m)
-        r = 1.0 / (jnp.sum(e1, axis=1, keepdims=True) + jnp.sum(e2, axis=1, keepdims=True))
-        return e1 * r, e2 * r
+        s1 = dot_nt(qb, kc) * INV2
+        s2 = jnp.where(causal, dot_nt(qb, k[rows, cols]) * INV2, NEG)
+        return s1, s2
 
     def fwd_head(h, c):
         cols = head_cols(h)
-        kc = cached(0, cols)
-        vc = cached(1, cols)
         for b in range(blocks):
             rows = pl.ds(b * BLOCK, BLOCK)
-            p1, p2 = probs_of(b, cols, kc)
-            o = dot_nn(p1.astype(BF16), vc) + dot_nn(p2.astype(BF16), v[rows, cols])
-            abuf[z, core, rows, cols] = o.astype(BF16)
+            s1, s2 = scores_of(rows, cols, listed(0, b, cols))
+            m = jnp.maximum(jnp.max(s1, axis=1, keepdims=True), jnp.max(s2, axis=1, keepdims=True))
+            e1 = jnp.exp2(s1 - m)
+            e2 = jnp.exp2(s2 - m)
+            total = jnp.sum(e1, axis=1, keepdims=True) + jnp.sum(e2, axis=1, keepdims=True)
+            o = dot_nn(e1.astype(BF16), listed(1, b, cols)) + dot_nn(e2.astype(BF16), v[rows, cols])
+            abuf[z, core, rows, cols] = (o / total).astype(BF16)
+            lse[h, rows, :] = m + jnp.log2(total)
         return c
 
+    for b in range(blocks):
+        pscr[b, KB] = jnp.zeros((BLOCK, BLOCK), BF16)
+        dscr[b, KB] = jnp.zeros((BLOCK, BLOCK), BF16)
     lax.fori_loop(0, wid // HEAD_DIM, fwd_head, 0)
     line_own(abuf.at[z, core], abuf, a_sems)
 
@@ -412,35 +414,39 @@
         lax.fori_loop(0, blocks, total, 0)
 
         def head(j, c):
-            cols = head_cols(h * (half // HEAD_DIM) + j)
+            hd = h * (half // HEAD_DIM) + j
+            cols = head_cols(hd)
             jc = head_cols(j)
-            kc = cached(0, cols)
-            vc = cached(1, cols)
             for b in range(blocks):
                 rows = pl.ds(b * BLOCK, BLOCK)
-                p1, p2 = probs_of(b, cols, kc)
+                kc = listed(0, b, cols)
+                s1, s2 = scores_of(rows, cols, kc)
+                norm = lse[hd, rows, :]
+                p1 = jnp.exp2(s1 - norm)
+                p2 = jnp.exp2(s2 - norm)
                 gb = ga[rows, jc]
-                d1 = dot_nt(gb, vc)
+                d1 = dot_nt(gb, listed(1, b, cols))
                 d2 = dot_nt(gb, v[rows, cols])
+                delta = jnp.sum(gb.astype(F32) * abuf[z, core, rows, cols].astype(F32), axis=1, keepdims=True)
                 b1 = p1.astype(BF16)
                 b2 = p2.astype(BF16)
-                delta = (jnp.sum(b1.astype(F32) * d1, axis=1, keepdims=True)
-                         + jnp.sum(b2.astype(F32) * d2, axis=1, keepdims=True))
                 t1 = (p1 * (d1 - delta)).astype(BF16)
                 t2 = (p2 * (d2 - delta)).astype(BF16)
-                pscr[rows, :] = b1
-                dscr[rows, :] = t1
+                for n in range(KB):
+                    pscr[b, n] = b1[:, n * BLOCK : (n + 1) * BLOCK]
+                    dscr[b, n] = t1[:, n * BLOCK : (n + 1) * BLOCK]
                 kb = k[rows, cols]
                 gq[rows, cols] = ((dot_nn(t1, kc) + dot_nn(t2, kb)) * INV).astype(BF16)
                 gk[rows, cols] = (dot_tn(t2, q[rows, cols]) * INV).astype(BF16)
                 gv[rows, cols] = dot_tn(b2, gb).astype(BF16)
-            ck = (dot_tn(dscr[...], q[:, cols]) * INV).astype(BF16)
-            cv = dot_tn(pscr[...], ga[:, jc]).astype(BF16)
-            for kv, part in ((0, ck), (1, cv)):
-                part = part.reshape(NZ, 2, BLOCK, HEAD_DIM)
-                for s in range(NZ):
-                    for side in range(2):
-                        cpart[h, side, s, kv, :, jc] = part[s, side]
+            qh = q[:, cols]
+            gh = ga[:, jc]
+            for s in range(NZ):
+                for side in range(2):
+                    ds = jnp.concatenate([dscr[b, slot_of[b, 2 * s + side]] for b in range(blocks)], axis=0)
+                    ps = jnp.concatenate([pscr[b, slot_of[b, 2 * s + side]] for b in range(blocks)], axis=0)
+                    cpart[h, side, s, 0, :, jc] = (dot_tn(ds, qh) * INV).astype(BF16)
+                    cpart[h, side, s, 1, :, jc] = dot_tn(ps, gh).astype(BF16)
             return c
 
         lax.fori_loop(0, half // HEAD_DIM, head, 0)
@@ -513,9 +519,9 @@
     for h in range(2):
         arrived(cbuf.at[h, z], s_rv.at[z, h], has_dn)
         arrived(cbuf.at[h, NZ], s_rv.at[NZ, h], has_up)
-        gc[:, :, pl.ds(h * half, half)] = (
-            cache_sum(h, z) + cbuf[h, z].astype(F32) + cbuf[h, NZ].astype(F32)
-        )
+        total = cache_sum(h, z) + cbuf[h, z].astype(F32) + cbuf[h, NZ].astype(F32)
+        gck[:, pl.ds(h * half, half)] = total[0]
+        gcv[:, pl.ds(h * half, half)] = total[1]
 
     for copy, cond in pending:
         when(cond, copy.wait_send)
@@ -527,8 +533,9 @@
     dblk = proj_weight.shape[0]
     blocks = tok // BLOCK
     cache = jnp.stack([cache_keys, cache_values])
-    named = jnp.any(block_table[:, :, None] == jnp.arange(CB, dtype=jnp.int32), axis=1)
-    bias = jnp.repeat(jnp.where(named, 0.0, NEG).astype(F32), BLOCK, axis=1).reshape(blocks, 1, CACHE)
+    match = block_table[:, :, None] == jnp.arange(CB, dtype=jnp.int32)
+    slot_of = KB - jnp.sum(match * (KB - jnp.arange(KB, dtype=jnp.int32))[None, :, None], axis=1)
+    sm = pl.BlockSpec(memory_space=pltpu.SMEM)
     vm = pl.BlockSpec(memory_space=pltpu.VMEM)
     hbm = pl.BlockSpec(memory_space=pl.ANY)
     dma = pltpu.SemaphoreType.DMA
@@ -538,13 +545,14 @@
             jax.ShapeDtypeStruct((tok, wid), BF16),
             jax.ShapeDtypeStruct((tok, wid), BF16),
             jax.ShapeDtypeStruct((tok, wid), BF16),
-            jax.ShapeDtypeStruct((2, BLOCK, wid), F32),
+            jax.ShapeDtypeStruct((BLOCK, wid), F32),
+            jax.ShapeDtypeStruct((BLOCK, wid), F32),
             jax.ShapeDtypeStruct((dblk, wid), BF16),
             jax.ShapeDtypeStruct((NZ, 2, BLOCK, dblk), BF16),
             jax.ShapeDtypeStruct((tok, dblk), BF16),
         ),
-        in_specs=[hbm, vm, hbm, vm, vm, vm, vm],
-        out_specs=[vm] * 5 + [hbm] * 2,
+        in_specs=[hbm, vm, hbm, vm, vm, vm, sm, sm, sm],
+        out_specs=[vm] * 6 + [hbm] * 2,
         scratch_shapes=[
             pltpu.VMEM((NZ, 2, 4, BLOCK, dblk), BF16),
             pltpu.VMEM((NZ, 2, 2, BLOCK, wid), BF16),
@@ -556,8 +564,9 @@
             pltpu.VMEM((2, 2, NZ, 2, BLOCK, half), BF16),
             pltpu.VMEM((2, NZ, 2, BLOCK, half), BF16),
             pltpu.VMEM((2, NZ + 1, 2, BLOCK, half), BF16),
-            pltpu.VMEM((tok, CACHE), BF16),
-            pltpu.VMEM((tok, CACHE), BF16),
+            pltpu.VMEM((blocks, KB + 1, BLOCK, BLOCK), BF16),
+            pltpu.VMEM((blocks, KB + 1, BLOCK, BLOCK), BF16),
+            pltpu.VMEM((wid // HEAD_DIM, tok, 1), F32),
             dma((4,)),
             dma((3,)), dma((3,)), dma((NZ,)), dma((7,)), dma((NZ,)),
             dma((3,)), dma((3,)), dma((NZ,)), dma((7,)), dma((NZ,)),
@@ -571,8 +580,8 @@
             collective_id=0, has_side_effects=True, vmem_limit_bytes=64 * 1024 * 1024
         ),
         name="fused",
-    )(grad_out, proj_weight, cache, queries, keys, values, bias)
-    return out[0], out[1], out[2], out[3][0], out[3][1], out[4]
+    )(grad_out, proj_weight, cache, queries, keys, values, block_table // 2, block_table % 2, slot_of)
+    return out[:6]
 
 
 def fits_fused(mesh):

time: 284 us -> 273 us (0.961)
  Pallas kernels: 272 us -> 260 us
    pallas_call x1, Pallas kernels: 272 us -> 260 us  [per_device_fused(): pl.pallas_call(fused_kernel, out_shape=(jax.ShapeDtypeStruct((tok, wid),...]
    unnamed x12 -> x16, local copies, waits for them, and re-layouts: 4.39 us -> 7.27 us
where the time goes in v3:
time: 273 us; the launch traced here: 272 us
  Pallas kernels  260 us (95%)
  local copies, waits for them, and re-layouts  7.27 us (3%)
  other arithmetic  4.5 us (2%)
    pallas_call x1, Pallas kernels, per_device_fused(): pl.pallas_call(fused_kernel, out_shape=(jax.ShapeDtypeStruct((tok, wid),...  260 us
    unnamed x16, local copies, waits for them, and re-layouts  7.27 us

profile of v3, /device:TPU:0, one launch (start us, length us, event | category | flops | bytes accessed | tf_op | source)
XLA Modules:
  0.0 272.5 jit_solution(17694455086799011602)
XLA Ops:
  0.6 0.8 select_reduce_fusion
  1.4 0.6 broadcast_subtract_fusion.slot_of
  2.0 1.3 add_select_fusion
  3.3 1.9 pad_maximum_fusion.cache
  5.1 260.1 %fused.1 = (bf16[512,1024]{1,0:T(8,128)(2,1)}, bf16[512,1024]{1,0:T(8,128)(2,1)}, bf16[512,1024]{1,0:T(8,128)(2,1)}, f32[128,1024]{1,0:T(8,128)}, f32[128,1024]{...) custom-call(bf16[512,2048]{1,0:T(8,128)(2,1)} %go.1, ...), custom_call_target="tpu_custom_call" | custom-call | tf_op jit(solution)/shard_map/fused/pallas_call | solution.py:542
  265.2 0.0 copy-start.2
  265.2 0.0 copy-start.1
  265.2 2.4 copy.20
  267.6 0.0 copy-done.2
  267.6 0.0 copy-start.4
  267.6 1.0 copy.21
  268.6 0.0 copy-done.1
  268.6 0.0 copy-start.3
  268.6 0.0 copy-start
  268.6 1.0 copy.22
  269.6 0.0 copy-done.4
  269.6 0.8 copy.23
  270.4 0.0 copy-done.3
  270.4 0.8 copy.24
  271.2 0.0 copy-done
  271.2 1.3 copy.25
  (1 shorter events, 0.0 us)
Async XLA Ops:
  265.2 2.4 copy-start.2
  265.2 3.4 %copy-start.1 = (bf16[512,1024]{1,0:T(8,128)(2,1)S(1)}, bf16[512,1024]{1,0:T(8,128)(2,1)}, u32[]{:S(2)}) copy-start(bf16[512,1024]{1,0:T(8,128)(2,1)} %get-tuple-element.28) | copy-start | bytes 3145732
  267.6 2.0 copy-start.4
  268.6 1.8 copy-start.3
  268.6 2.6 copy-start

commit v4 on v3

--- a/solution.py
+++ b/solution.py
@@ -208,7 +208,11 @@
     def greet(dev):
         pl.semaphore_signal(barrier, inc=1, device_id=dev, device_id_type=pl.DeviceIdType.MESH)
 
-    zs_of = [(z + NZ - i) % NZ for i in range(NZ)]
+    zs_of = [z]
+    for i in range(1, NZ):
+        high = jnp.where(NZ - i > z, NZ - i, NZ - i - 1)
+        low = jnp.where(i - 1 < z, i - 1, i)
+        zs_of.append(jnp.where(z < NZ // 2, high, low))
     zd_of = [(z + i) % NZ for i in range(NZ)]
     line = [{"col": zd_of[i] * 2 + core} for i in range(NZ)]
     for dev in (partner, xn, yn, dg, line[1], line[2], line[3]):
@@ -277,7 +281,6 @@
         send(rcopy(gx.at[quarter(r)], H.at[row, other], g_s.at[4 + n], g_r.at[1 + 2 * n + other], dev))
     own_gx = pltpu.make_async_copy(gx.at[quarter(row)], H.at[row, other], loc_sem.at[2])
     own_gx.start()
-    line_step(2, ckv, c_sems)
     for c in locals_:
         c.wait()
     own_gx.wait()
@@ -287,14 +290,14 @@
     own_h = pltpu.make_async_copy(H.at[z], G.at[z, :, row], loc_sem.at[3])
     own_h.start()
     for i in range(1, NZ):
-        send(rcopy(H.at[zd_of[i]], G.at[z, :, row], g_s.at[6 + i], g_r.at[6 + i], line[i]))
+        send(rcopy(H.at[zd_of[i]], G.at[z, :, row], g_s.at[6 + i], g_r.at[26 + z], line[i]))
 
     def plane_send(i):
         piece = G.at[zs_of[i], :, row]
         if i == 0:
             own_h.wait()
         else:
-            arrived(piece, g_r.at[6 + i])
+            arrived(piece, g_r.at[26 + zs_of[i]])
         send(rcopy(piece, piece, g_s.at[10 + i], g_r.at[10 + i], xn))
         send(rcopy(piece, piece, g_s.at[14 + i], g_r.at[14 + i], yn))
 
@@ -305,6 +308,7 @@
         arrived(G.at[zs, :, ry], g_r.at[14 + i])
         send(rcopy(G.at[zs, 1, ry], G.at[zs, 1, ry], g_s.at[22 + i], g_r.at[22 + i], xn))
 
+    line_step(2, ckv, c_sems)
     plane_send(0)
     line_step(3, ckv, c_sems)
     for s in range(NZ):
@@ -477,32 +481,38 @@
 
             send(rcopy(cbuf.at[h, s], cbuf.at[h, dst], sems.at[t, h], s_rv.at[dst, h], dev), go_)
 
+    def ga_swap(i):
+        arrived(grecv.at[zs_of[i]], p_r.at[i])
+
     plane_send(1)
     plane_pass(0)
     line_step(1, abuf, a_sems)
     plane_send(2)
-    ga_part(0)
     plane_pass(1)
     plane_send(3)
     ga_part(1)
+    ga_part(0)
+    ga_swap(1)
+    rs_step(0, 0)
+    rs_step(0, 1)
     plane_pass(2)
-    line_step(2, abuf, a_sems)
     ga_part(2)
     plane_pass(3)
     ga_part(3)
-    for i in range(NZ):
-        arrived(grecv.at[zs_of[i]], p_r.at[i])
-    rs_step(0, 0)
-    rs_step(0, 1)
-    line_step(3, abuf, a_sems)
+    ga_swap(2)
+    line_step(2, abuf, a_sems)
     rs_step(1, 0)
     rs_step(1, 1)
+    ga_swap(3)
+    ga_swap(0)
+    line_step(3, abuf, a_sems)
     for s in range(NZ):
         arrived(abuf.at[s, other], a_pr.at[s])
     gw_tile(0)
     rs_step(2, 0)
+    rs_step(2, 1)
     gw_tile(1)
-    rs_step(2, 1)
+    gw_tile(2)
     bwd(0)
     pair_sum(0)
     crs_step(0, 0)
@@ -511,9 +521,8 @@
     pair_sum(1)
     crs_step(0, 1)
     crs_step(2, 0)
-    gw_tile(2)
+    gw_tile(3)
     crs_step(1, 1)
-    gw_tile(3)
     crs_step(2, 1)
 
     for h in range(2):
@@ -570,7 +579,7 @@
             dma((4,)),
             dma((3,)), dma((3,)), dma((NZ,)), dma((7,)), dma((NZ,)),
             dma((3,)), dma((3,)), dma((NZ,)), dma((7,)), dma((NZ,)),
-            dma((26,)), dma((26,)),
+            dma((26,)), dma((26 + NZ,)),
             dma((NZ,)), dma((NZ,)),
             dma((2,)), dma((2,)),
             dma((3, 2)), dma((3, 2)), dma((NZ + 1, 2)),

time: 273 us -> 274 us (level)
  no operation moved by 1% of the time
where the time goes in v4:
time: 274 us
  Pallas kernels  262 us (96%)
  local copies, waits for them, and re-layouts  7.27 us (3%)
  other arithmetic  4.5 us (2%)
    pallas_call x1, Pallas kernels, per_device_fused(): pl.pallas_call(fused_kernel, out_shape=(jax.ShapeDtypeStruct((tok, wid),...  262 us
    unnamed x16, local copies, waits for them, and re-layouts  7.27 us

profile of v4, /device:TPU:0, one launch (start us, length us, event | category | flops | bytes accessed | tf_op | source)
XLA Modules:
  0.0 274.0 jit_solution(3601634364247744507)
XLA Ops:
  0.6 0.8 select_reduce_fusion
  1.4 0.6 broadcast_subtract_fusion.slot_of
  2.0 1.3 add_select_fusion
  3.3 1.9 pad_maximum_fusion.cache
  5.1 261.5 %fused.1 = (bf16[512,1024]{1,0:T(8,128)(2,1)}, bf16[512,1024]{1,0:T(8,128)(2,1)}, bf16[512,1024]{1,0:T(8,128)(2,1)}, f32[128,1024]{1,0:T(8,128)}, f32[128,1024]{...) custom-call(bf16[512,2048]{1,0:T(8,128)(2,1)} %go.1, ...), custom_call_target="tpu_custom_call" | custom-call | tf_op jit(solution)/shard_map/fused/pallas_call | solution.py:551
  266.7 0.0 copy-start.2
  266.7 0.0 copy-start.1
  266.7 2.4 copy.20
  269.1 0.0 copy-done.2
  269.1 0.0 copy-start.4
  269.1 1.0 copy.21
  270.1 0.0 copy-done.1
  270.1 0.0 copy-start.3
  270.1 0.0 copy-start
  270.1 1.0 copy.22
  271.1 0.0 copy-done.4
  271.1 0.8 copy.23
  271.9 0.0 copy-done.3
  271.9 0.8 copy.24
  272.7 0.0 copy-done
  272.7 1.3 copy.25
  (1 shorter events, 0.0 us)
Async XLA Ops:
  266.7 2.4 copy-start.2
  266.7 3.4 %copy-start.1 = (bf16[512,1024]{1,0:T(8,128)(2,1)S(1)}, bf16[512,1024]{1,0:T(8,128)(2,1)}, u32[]{:S(2)}) copy-start(bf16[512,1024]{1,0:T(8,128)(2,1)} %get-tuple-element.28) | copy-start | bytes 3145732
  269.1 2.0 copy-start.4
  270.1 1.8 copy-start.3
  270.1 2.6 copy-start
